TPU v7x, 512 devices: a whole 4x4x16 slice. The times are simulated.
512 devices in a mesh: gx: 32 (over z, core), gy: 16 (over y, x).
Axes of the slice: x: 4, y: 4, z: 16, core: 2. Of those that a mesh axis runs over, the one named last changes fastest.
Arguments:
- solution: float32 [512, 65536], P(None, ('gx', 'gy')), may hold values from -6 to 6
- residual: float32 [512, 65536], P(None, ('gx', 'gy')), may hold values from -60 to 60
- metric_diag: bfloat16 [3, 512, 65536], P(None, None, ('gx', 'gy')), may hold values from 0.039794922 to 0.3984375
- metric_cross: bfloat16 [3, 512, 65536], P(None, None, ('gx', 'gy')), may hold values from -0.017944336 to 0.017944336
- fdm_vectors: float32 [3, 8, 8, 65536], P(None, None, None, ('gx', 'gy')), may hold values from -5 to 5
- fdm_values: float32 [3, 8, 65536], P(None, None, ('gx', 'gy')), may hold values from 0.05 to 20
- vertex_ids: int32 [8, 65536], P(None, ('gx', 'gy')), may hold values from 0 to 8191
- coarse_inverse: float32 [8192, 8192], P(('gx', 'gy')), may hold values from -0.2 to 0.2, as said below
- elem_live: int32 [512], P(('gx', 'gy')), may hold values from 80 to 128, as said below
- section_face: int32 [512, 16, 20], P(('gx', 'gy')), may hold values from -1 to 767, as said below
- section_code: int32 [512, 16, 20], P(('gx', 'gy')), may hold values from 0 to 7, as said below
- pipe_face: int32 [512, 2, 64], P(('gx', 'gy')), may hold values from 0 to 767, as said below
- pipe_code: int32 [512, 2, 64], P(('gx', 'gy')), may hold values from 0 to 7, as said below
Outputs:
- solution_out: float32 [512, 65536], P(None, ('gx', 'gy'))
- residual_out: float32 [512, 65536], P(None, ('gx', 'gy'))
- norm_ratio: float32 [1], replicated
Inputs may be any that keep to these rules, and one draw needn't show every extreme that they name: `elem_live`: one device holds all 128 slots in every draw. A face id 6 e + f names face f of slot e of the device, with e below the device's elem_live; no id appears twice on a device over section_face and pipe_face; -1 marks an empty slot, and in each peer's row the slots holding faces come first. Slot (q, c) of device (x, y) holds a face exactly when slot (y, c) of device (x, q) does; in the row q = y they come in pairs (c, c xor 1). Each device's rows for peers y - 1, y + 1 and y + 16 / 2 (mod 16) are full; rows for other peers more than two places away (mod 16) are empty. `section_code`: with inv(o) = o for o < 4 and 4 + 2 (o mod 2) + floor((o mod 4) / 2) for o >= 4, the codes of two paired slots are inv of each other; empty slots hold 0. `pipe_face`: every slot holds a face, as for section_face. `pipe_code`: the codes of two paired slots are inv of each other, as for section_code. `coarse_inverse`: Symmetric.
All inputs are finite; a program needn't handle non-finite values.
Results may differ from a plain program's by a relative error of at most 0.0003.
Values sent between devices are 32-bit elements; how exact they have to be, the bound alone decides.
A program may use at most 64 MiB of HBM per device.

v0:
```python
import jax
import jax.numpy as jnp
from jax import lax
from jax.sharding import PartitionSpec as P

EDGE = 8
top_precision = lax.Precision.HIGHEST


def padded(block, sides, width):
    for axis, dim in sides:
        count = lax.axis_size(axis)
        forward = [(i, i + 1) for i in range(count - 1)]
        forward.append((count - 1, 0))
        backward = [(target, source) for source, target in forward]
        low = lax.ppermute(
            lax.slice_in_dim(block, block.shape[dim] - width, None, axis=dim), axis, forward
        )
        high = lax.ppermute(lax.slice_in_dim(block, 0, width, axis=dim), axis, backward)
        block = jnp.concatenate([low, block, high], axis=dim)
    return block


def node_points():
    node_index = jnp.arange(EDGE).astype(jnp.float32)
    return -jnp.cos(jnp.pi * node_index / (EDGE - 1))


def derivative_matrix():
    points = node_points()
    node_index = jnp.arange(EDGE)
    weights = jnp.where((node_index == 0) | (node_index == EDGE - 1), 2.0, 1.0).astype(jnp.float32)
    parity = jnp.where((node_index[:, None] + node_index[None, :]) % 2 == 0, 1.0, -1.0).astype(
        jnp.float32
    )
    identity = jnp.eye(EDGE, dtype=jnp.float32)
    spacing = points[:, None] - points[None, :] + identity
    offdiag = weights[:, None] / weights[None, :] * parity / spacing * (1.0 - identity)
    return offdiag - jnp.diag(jnp.sum(offdiag, axis=1))


def corner_table():
    points = node_points()
    hat_values = jnp.stack([(1.0 - points) * 0.5, (1.0 + points) * 0.5])
    corner_weights = (
        hat_values[:, None, None, :, None, None]
        * hat_values[None, :, None, None, :, None]
        * hat_values[None, None, :, None, None, :]
    )
    return corner_weights.reshape(8, EDGE**3)


def contract(matrices, element_cube, axis):
    moved = jnp.moveaxis(element_cube, axis, 0)
    total = matrices[0][:, None, None, :] * moved[0][None]
    for index in range(1, EDGE):
        total = total + matrices[index][:, None, None, :] * moved[index][None]
    return jnp.moveaxis(total, 0, axis)


def orient_columns(face_cols, orient_codes):
    face_grid = face_cols.reshape(EDGE, EDGE, -1)
    face_grid = jnp.where((orient_codes % 2 == 1)[None, None, :], face_grid[::-1, :, :], face_grid)
    face_grid = jnp.where(
        (orient_codes // 2 % 2 == 1)[None, None, :], face_grid[:, ::-1, :], face_grid
    )
    face_grid = jnp.where(
        (orient_codes >= 4)[None, None, :], jnp.swapaxes(face_grid, 0, 1), face_grid
    )
    return face_grid.reshape(EDGE * EDGE, -1)


def fdm_solve(element_cube, vectors, values):
    spectral = contract(vectors[0], element_cube, 0)
    spectral = contract(vectors[1], spectral, 1)
    spectral = contract(vectors[2], spectral, 2)
    eigen_sums = (
        values[0][:, None, None, :] + values[1][None, :, None, :] + values[2][None, None, :, :]
    )
    spectral = spectral / eigen_sums
    restored = contract(jnp.swapaxes(vectors[0], 0, 1), spectral, 0)
    restored = contract(jnp.swapaxes(vectors[1], 0, 1), restored, 1)
    return contract(jnp.swapaxes(vectors[2], 0, 1), restored, 2)


def local_operator(field, diag_part, cross_part, derivative):
    element_cube = field.reshape(EDGE, EDGE, EDGE, -1)
    diagonal = diag_part.astype(jnp.float32).reshape(3, EDGE, EDGE, EDGE, -1)
    cross_terms = cross_part.astype(jnp.float32).reshape(3, EDGE, EDGE, EDGE, -1)
    forward = jnp.transpose(derivative)[:, :, None]
    backward = derivative[:, :, None]
    grad_first = contract(forward, element_cube, 0)
    grad_second = contract(forward, element_cube, 1)
    grad_third = contract(forward, element_cube, 2)
    flux_first = (
        diagonal[0] * grad_first + cross_terms[0] * grad_second + cross_terms[1] * grad_third
    )
    flux_second = (
        cross_terms[0] * grad_first + diagonal[1] * grad_second + cross_terms[2] * grad_third
    )
    flux_third = (
        cross_terms[1] * grad_first + cross_terms[2] * grad_second + diagonal[2] * grad_third
    )
    curvature = jnp.sum(
        grad_first * flux_first + grad_second * flux_second + grad_third * flux_third
    ) + jnp.sum(element_cube * element_cube)
    applied = contract(backward, flux_first, 0)
    applied = applied + contract(backward, flux_second, 1)
    applied = applied + contract(backward, flux_third, 2)
    return ((applied + element_cube).reshape(EDGE**3, -1), curvature)


def face_sum(field, section_face, section_code, pipe_face, pipe_code):
    element_cube = field.reshape(EDGE, EDGE, EDGE, -1)
    slot_count = element_cube.shape[3]
    stacked = jnp.stack(
        [
            element_cube[0],
            element_cube[EDGE - 1],
            element_cube[:, 0],
            element_cube[:, EDGE - 1],
            element_cube[:, :, 0],
            element_cube[:, :, EDGE - 1],
        ],
        axis=-1,
    )
    face_values = stacked.reshape(EDGE * EDGE, slot_count * 6)
    face_count = face_values.shape[1]
    peer_count = section_face.shape[1]
    capacity = section_face.shape[2]
    wanted = section_face[0].reshape(-1)
    picked = jnp.take(face_values, jnp.maximum(wanted, 0), axis=1)
    outgoing = jnp.where((wanted >= 0)[None, :], picked, 0.0).reshape(
        EDGE * EDGE, peer_count, capacity
    )
    own_index = lax.axis_index("gy")
    arrived = lax.all_to_all(outgoing, "gy", split_axis=1, concat_axis=1, tiled=True)
    swapped = arrived.reshape(EDGE * EDGE, peer_count, capacity // 2, 2)[..., ::-1].reshape(
        EDGE * EDGE, peer_count, capacity
    )
    arrived = jnp.where((jnp.arange(peer_count) == own_index)[None, :, None], swapped, arrived)
    incoming = orient_columns(
        arrived.reshape(EDGE * EDGE, peer_count * capacity), section_code[0].reshape(-1)
    )
    pipe_ids = pipe_face[0]
    pipe_width = pipe_ids.shape[1]
    boundary = jnp.take(face_values, pipe_ids.reshape(-1), axis=1).reshape(
        EDGE * EDGE, 2, pipe_width
    )
    extended = padded(boundary, (("gx", 1),), 1)
    beside = jnp.concatenate([extended[:, 0], extended[:, 3]], axis=1)
    beside = orient_columns(beside, pipe_code[0].reshape(-1))
    targets = jnp.concatenate([wanted, pipe_ids.reshape(-1)])
    placed = jnp.where(targets < 0, face_count, targets)
    face_extra = (
        jnp.zeros((EDGE * EDGE, face_count), jnp.float32)
        .at[:, placed]
        .add(jnp.concatenate([incoming, beside], axis=1), mode="drop")
    )
    face_parts = face_extra.reshape(EDGE, EDGE, slot_count, 6)
    element_cube = element_cube.at[0].add(face_parts[..., 0])
    element_cube = element_cube.at[EDGE - 1].add(face_parts[..., 1])
    element_cube = element_cube.at[:, 0].add(face_parts[..., 2])
    element_cube = element_cube.at[:, EDGE - 1].add(face_parts[..., 3])
    element_cube = element_cube.at[:, :, 0].add(face_parts[..., 4])
    element_cube = element_cube.at[:, :, EDGE - 1].add(face_parts[..., 5])
    return element_cube.reshape(EDGE**3, -1)


def on_device(
    solution,
    residual,
    metric_diag,
    metric_cross,
    fdm_vectors,
    fdm_values,
    vertex_ids,
    coarse_inverse,
    elem_live,
    section_face,
    section_code,
    pipe_face,
    pipe_code,
):
    slot_count = residual.shape[1]
    alive_mask = (jnp.arange(slot_count) < elem_live[0]).astype(jnp.float32)
    rmask = residual * alive_mask[None, :]
    corner_weights = corner_table()
    derivative = derivative_matrix()
    corners = jnp.dot(corner_weights, rmask, precision=top_precision)
    coarse_partial = jax.ops.segment_sum(
        corners.reshape(-1), vertex_ids.reshape(-1), num_segments=coarse_inverse.shape[1]
    )
    coarse_rhs = lax.psum(coarse_partial, ("gx", "gy"))
    own_values = jnp.dot(coarse_inverse, coarse_rhs, precision=top_precision)
    coarse_sol = lax.all_gather(own_values, ("gx", "gy"), axis=0, tiled=True)
    smooth = fdm_solve(rmask.reshape(EDGE, EDGE, EDGE, -1), fdm_vectors, fdm_values).reshape(
        EDGE**3, -1
    )
    summed = face_sum(smooth, section_face, section_code, pipe_face, pipe_code)
    lifted = jnp.dot(corner_weights.T, coarse_sol[vertex_ids], precision=top_precision)
    direction = alive_mask[None, :] * (summed + lifted)
    applied, curvature_local = local_operator(direction, metric_diag, metric_cross, derivative)
    image = face_sum(applied, section_face, section_code, pipe_face, pipe_code)
    precond_local = jnp.sum(rmask * direction)
    norm_local = jnp.sum(rmask * rmask)
    precond_dot, curvature, old_norm = lax.psum(
        (precond_local, curvature_local, norm_local), ("gx", "gy")
    )
    step_length = precond_dot / curvature
    residual_out = rmask - step_length * image
    fresh_norm = lax.psum(jnp.sum(residual_out * residual_out), ("gx", "gy"))
    solution_out = alive_mask[None, :] * (solution + step_length * direction)
    norm_ratio = (fresh_norm / old_norm).reshape(1)
    return (solution_out, residual_out, norm_ratio)


def solution(mesh):
    placed = (
        P(None, ("gx", "gy")),
        P(None, ("gx", "gy")),
        P(None, None, ("gx", "gy")),
        P(None, None, ("gx", "gy")),
        P(None, None, None, ("gx", "gy")),
        P(None, None, ("gx", "gy")),
        P(None, ("gx", "gy")),
        P(("gx", "gy"), None),
        P(("gx", "gy")),
        P(("gx", "gy"), None, None),
        P(("gx", "gy"), None, None),
        P(("gx", "gy"), None, None),
        P(("gx", "gy"), None, None),
    )
    return jax.shard_map(
        on_device,
        mesh=mesh,
        in_specs=placed,
        out_specs=(P(None, ("gx", "gy")), P(None, ("gx", "gy")), P()),
        check_vma=False,
    )
```

profile of v0, /device:TPU:1, one launch (start us, length us, event | category | flops | bytes accessed | tf_op | source)
XLA Modules:
  0.0 567.3 jit_solution(12377010773833954774)
XLA Ops:
  6.8 2.3 copy.389
  9.0 2.5 reshape.1869
  14.6 7.6 %all-to-all-start = ((f32[16,1,1280]{2,1,0:T(1,128)}), f32[16,1,1280]{2,1,0:T(1,128)}, u32[]{:S(2)}, u32[]{:S(2)}) async-start(f32[16,1,1280]{2,1,0:T(1,128)} %reshape.1990), calls=%async_computation | async-start | bytes 163840 | tf_op jit(solution)/shard_map/all_to_all | solution.py:137
  23.7 2.5 collective-permute-start
  30.1 5.9 %scatter_custom_fusion.1 = f32[8192]{0:T(1024)S(1)} fusion(s32[1024]{0:T(1024)S(1)} %bitcast.649, f32[1024]{0:T(1024)S(1)} %convolution_bitcast_fusion, f32[]{:T(128)} %constant.402.clone.1), kind=kCustom, calls=%fused_computation.199 | custom fusion | flops 1024 | bytes 32772 | tf_op jit(solution)/shard_map/scatter-add | solution.py:191
  36.1 108.5 %psum.35 = f32[8192]{0:T(1024)S(1)} all-reduce(f32[8192]{0:T(1024)S(1)} %scatter_custom_fusion.1), channel_id=1, replica_groups=mesh['gx'=32,'gy'=16] {'gx','gy'}, use_global_device_ids=true, to_apply=%region_2.5 | all-reduce | flops 8192 | bytes 65536 | tf_op jit(solution)/shard_map/psum | solution.py:194
  169.9 99.5 %all-reduce = f32[8192]{0:T(1024)S(1)} all-reduce(f32[8192]{0:T(1024)S(1)} %dynamic-update-slice.36), channel_id=1, replica_groups=mesh['gx'=32,'gy'=16] {'gx','gy'}, use_global_device_ids=true, to_apply=%add | all-reduce | flops 8192 | bytes 65536
  269.4 10.5 %gather_fusion = f32[1024]{0:T(1024)} fusion(f32[8192]{0:T(1024)S(1)} %all-reduce, s32[1024]{0:T(1024)S(1)} %fusion.40), kind=kCustom, calls=%fused_computation.4 | custom fusion | bytes 12288 | tf_op jit(solution)/shard_map/gather | solution.py:201
  280.6 1.6 reduce.26
  283.5 2.3 scatter_custom_fusion
  285.7 2.6 reshape.1876
  288.4 3.4 fusion.54
  291.8 1.9 copy.456
  294.4 1.3 copy.401
  295.7 1.2 copy.403
  298.1 1.2 copy.459
  301.8 2.0 multiply_reduce_fusion
  304.4 1.5 multiply_add_fusion
  306.1 1.5 add_bitcast_fusion.1
  309.7 2.3 copy.428
  312.0 2.4 reshape.1886
  317.3 4.2 all-to-all-start.1
  322.3 1.8 collective-permute-start.2
  339.6 2.9 add_reduce_fusion
  343.7 102.5 %all-reduce.2 = (f32[]{:T(128)}, f32[]{:T(128)}) all-reduce(f32[]{:T(128)} %get-tuple-element.150, f32[]{:T(128)S(6)} %add.970), channel_id=1, replica_groups=mesh['gx'=32,'gy'=16] {'gx','gy'}, use_global_device_ids=true, to_apply=%region_4.7 | all-reduce | flops 2 | bytes 16 | tf_op jit(solution)/shard_map/psum | solution.py:207
  447.6 1.7 add_multiply_fusion
  450.2 1.6 reduce.27
  453.1 2.5 scatter_custom_fusion.2
  455.7 2.6 reshape.1893
  458.3 2.9 fusion.53
  464.1 1.3 multiply_reduce_fusion.1
  465.4 99.4 %all-reduce.1 = (f32[]{:T(128)}, f32[]{:T(128)}) all-reduce(f32[]{:T(128)} %get-tuple-element.156, f32[]{:T(128)} %get-tuple-element.149), channel_id=1, replica_groups=mesh['gx'=32,'gy'=16] {'gx','gy'}, use_global_device_ids=true, to_apply=%region_11.14 | all-reduce | flops 2 | bytes 16 | tf_op jit(solution)/shard_map/psum | solution.py:212
  (515 shorter events, 70.4 us)
Async XLA Ops:
  0.6 147.6 %copy-start = (f32[16,8192]{1,0:T(8,128)S(1)}, f32[16,8192]{1,0:T(8,128)}, u32[]{:S(2)}) copy-start(f32[16,8192]{1,0:T(8,128)} %param.48) | copy-start | bytes 1572868
  9.0 21.1 %copy-start.121 = (s32[8,128]{1,0:T(8,128)S(1)}, s32[8,128]{1,0:T(8,128)}, u32[]{:S(2)}) copy-start(s32[8,128]{1,0:T(8,128)} %param.47) | copy-start | bytes 12292
  9.0 135.9 %copy-start.2 = (bf16[3,512,128]{2,1,0:T(8,128)(2,1)S(1)}, bf16[3,512,128]{2,1,0:T(8,128)(2,1)}, u32[]{:S(2)}) copy-start(bf16[3,512,128]{2,1,0:T(8,128)(2,1)} %param.44) | copy-start | bytes 1179652
  11.5 134.5 %copy-start.1 = (bf16[3,512,128]{2,1,0:T(8,128)(2,1)S(1)}, bf16[3,512,128]{2,1,0:T(8,128)(2,1)}, u32[]{:S(2)}) copy-start(bf16[3,512,128]{2,1,0:T(8,128)(2,1)} %param.43) | copy-start | bytes 1179652
  12.5 134.4 %copy-start.110 = (s32[1024]{0:T(1024)}, s32[1024]{0:T(1024)S(1)}, u32[]{:S(2)}) copy-start(s32[1024]{0:T(1024)S(1)} %get-tuple-element.373) | copy-start | bytes 12292
  14.6 265.5 %all-to-all-start = ((f32[16,1,1280]{2,1,0:T(1,128)}), f32[16,1,1280]{2,1,0:T(1,128)}, u32[]{:S(2)}, u32[]{:S(2)}) async-start(f32[16,1,1280]{2,1,0:T(1,128)} %reshape.1990), calls=%async_computation | async-start | bytes 163840 | tf_op jit(solution)/shard_map/all_to_all | solution.py:137
  23.5 256.5 %copy-start.66 = (pred[128]{0:T(512)(128)(4,1)}, pred[128]{0:T(512)(128)(4,1)S(1)}, u32[]{:S(2)}) copy-start(pred[128]{0:T(512)(128)(4,1)S(1)} %get-tuple-element.360) | copy-start | bytes 388
  23.7 256.2 %collective-permute-start = (f32[64,1,64]{2,0,1:T(8,128)S(1)}, f32[64,1,64]{2,0,1:T(8,128)S(1)}, u32[]{:S(2)}, u32[]{:S(2)}) collective-permute-start(f32[64,1,64]{2,0,1:T(8,128)S(1)} %copy.454), channel_id=1, source_target_pairs={{0,16},{16,32},{32,48},{48,64},{64,80},{80,96},{96,112},{112,128},... | collective-permute-start | bytes 49160 | tf_op jit(solution)/shard_map/ppermute | solution.py:16
  26.8 253.1 %collective-permute-start.1 = (f32[64,1,64]{2,0,1:T(8,128)}, f32[64,1,64]{2,0,1:T(8,128)S(1)}, u32[]{:S(2)}, u32[]{:S(2)}) collective-permute-start(f32[64,1,64]{2,0,1:T(8,128)} %copy.455), channel_id=1, source_target_pairs={{16,0},{32,16},{48,32},{64,48},{80,64},{96,80},{112,96},{128,112},... | collective-permute-start | bytes 49160 | tf_op jit(solution)/shard_map/ppermute | solution.py:19
  144.9 19.5 %copy-start.42 = (f32[8]{0:T(128)}, f32[8]{0:T(128)S(1)}, u32[]{:S(2)}) copy-start(f32[8]{0:T(128)S(1)} %get-tuple-element.346) | copy-start | bytes 100
  144.9 20.1 %copy-start.56 = (f32[8]{0:T(128)}, f32[8]{0:T(128)S(1)}, u32[]{:S(2)}) copy-start(f32[8]{0:T(128)S(1)} %get-tuple-element.353) | copy-start | bytes 100
  144.9 20.8 %copy-start.54 = (f32[8]{0:T(128)}, f32[8]{0:T(128)S(1)}, u32[]{:S(2)}) copy-start(f32[8]{0:T(128)S(1)} %get-tuple-element.352) | copy-start | bytes 100
  144.9 21.4 %copy-start.52 = (f32[8]{0:T(128)}, f32[8]{0:T(128)S(1)}, u32[]{:S(2)}) copy-start(f32[8]{0:T(128)S(1)} %get-tuple-element.351) | copy-start | bytes 100
  144.9 22.1 %copy-start.50 = (f32[8]{0:T(128)}, f32[8]{0:T(128)S(1)}, u32[]{:S(2)}) copy-start(f32[8]{0:T(128)S(1)} %get-tuple-element.350) | copy-start | bytes 100
  144.9 22.8 %copy-start.48 = (f32[8]{0:T(128)}, f32[8]{0:T(128)S(1)}, u32[]{:S(2)}) copy-start(f32[8]{0:T(128)S(1)} %get-tuple-element.349) | copy-start | bytes 100
  144.9 23.5 %copy-start.46 = (f32[8]{0:T(128)}, f32[8]{0:T(128)S(1)}, u32[]{:S(2)}) copy-start(f32[8]{0:T(128)S(1)} %get-tuple-element.348) | copy-start | bytes 100
  145.0 24.1 %copy-start.44 = (f32[8]{0:T(128)}, f32[8]{0:T(128)S(1)}, u32[]{:S(2)}) copy-start(f32[8]{0:T(128)S(1)} %get-tuple-element.347) | copy-start | bytes 100
  152.5 127.5 %copy-start.83 = (pred[128]{0:T(512)(128)(4,1)S(1)}, pred[128]{0:T(512)(128)(4,1)}, u32[]{:S(2)}) copy-start(pred[128]{0:T(512)(128)(4,1)} %get-tuple-element.361) | copy-start | bytes 388
  152.6 127.5 %copy-start.117 = (pred[128]{0:T(512)(128)(4,1)S(1)}, pred[128]{0:T(512)(128)(4,1)}, u32[]{:S(2)}) copy-start(pred[128]{0:T(512)(128)(4,1)} %get-tuple-element.359) | copy-start | bytes 388
  165.0 117.4 %copy-start.122 = (pred[16]{0:T(512)(128)(4,1)S(1)}, pred[16]{0:T(512)(128)(4,1)}, u32[]{:S(2)}) copy-start(pred[16]{0:T(512)(128)(4,1)} %iota_compare_fusion.2) | copy-start | bytes 52
  317.3 132.9 %all-to-all-start.1 = ((f32[16,1,1280]{2,1,0:T(1,128)}), f32[16,1,1280]{2,1,0:T(1,128)}, u32[]{:S(2)}, u32[]{:S(2)}) async-start(f32[16,1,1280]{2,1,0:T(1,128)} %reshape.1992), calls=%async_computation.1 | async-start | bytes 163840 | tf_op jit(solution)/shard_map/all_to_all | solution.py:137
  321.4 17.7 %copy-start.19 = (f32[1,8,8,128]{3,0,2,1:T(1,128)S(1)}, f32[1,8,8,128]{3,0,2,1:T(1,128)}, u32[]{:S(2)}) copy-start(f32[1,8,8,128]{3,0,2,1:T(1,128)} %copy-done.18) | copy-start | bytes 98308
  322.3 127.0 %collective-permute-start.2 = (f32[64,1,64]{2,0,1:T(8,128)}, f32[64,1,64]{2,0,1:T(8,128)}, u32[]{:S(2)}, u32[]{:S(2)}) collective-permute-start(f32[64,1,64]{2,0,1:T(8,128)} %copy.460), channel_id=1, source_target_pairs={{0,16},{16,32},{32,48},{48,64},{64,80},{80,96},{96,112},{112,128},... | collective-permute-start | bytes 49160 | tf_op jit(solution)/shard_map/ppermute | solution.py:16
  324.8 124.5 %collective-permute-start.3 = (f32[64,1,64]{2,0,1:T(8,128)}, f32[64,1,64]{2,0,1:T(8,128)}, u32[]{:S(2)}, u32[]{:S(2)}) collective-permute-start(f32[64,1,64]{2,0,1:T(8,128)} %copy.461), channel_id=1, source_target_pairs={{16,0},{32,16},{48,32},{64,48},{80,64},{96,80},{112,96},{128,112},... | collective-permute-start | bytes 49160 | tf_op jit(solution)/shard_map/ppermute | solution.py:19
  339.5 108.0 %copy-start.72 = (f32[128]{0:T(128)S(1)}, f32[128]{0:T(128)}, u32[]{:S(2)}) copy-start(f32[128]{0:T(128)} %copy-done.71) | copy-start | bytes 1540
  339.5 110.6 %copy-start.67 = (pred[128]{0:T(512)(128)(4,1)S(1)}, pred[128]{0:T(512)(128)(4,1)}, u32[]{:S(2)}) copy-start(pred[128]{0:T(512)(128)(4,1)} %copy-done.66) | copy-start | bytes 388
  339.6 110.6 %copy-start.84 = (pred[128]{0:T(512)(128)(4,1)S(1)}, pred[128]{0:T(512)(128)(4,1)}, u32[]{:S(2)}) copy-start(pred[128]{0:T(512)(128)(4,1)} %get-tuple-element.361) | copy-start | bytes 388
  339.6 110.6 %copy-start.118 = (pred[128]{0:T(512)(128)(4,1)S(1)}, pred[128]{0:T(512)(128)(4,1)}, u32[]{:S(2)}) copy-start(pred[128]{0:T(512)(128)(4,1)} %get-tuple-element.359) | copy-start | bytes 388
  339.6 112.4 %copy-start.123 = (pred[16]{0:T(512)(128)(4,1)S(1)}, pred[16]{0:T(512)(128)(4,1)}, u32[]{:S(2)}) copy-start(pred[16]{0:T(512)(128)(4,1)} %iota_compare_fusion.2) | copy-start | bytes 52
  342.5 110.2 %copy-start.65 = (pred[320]{0:T(512)(128)(4,1)S(1)}, pred[320]{0:T(512)(128)(4,1)}, u32[]{:S(2)}) copy-start(pred[320]{0:T(512)(128)(4,1)} %get-tuple-element.355) | copy-start | bytes 964
  342.5 110.4 %copy-start.74 = (pred[320]{0:T(512)(128)(4,1)S(1)}, pred[320]{0:T(512)(128)(4,1)}, u32[]{:S(2)}) copy-start(pred[320]{0:T(512)(128)(4,1)} %get-tuple-element.356) | copy-start | bytes 964
  342.5 110.4 %copy-start.112 = (pred[320]{0:T(512)(128)(4,1)S(1)}, pred[320]{0:T(512)(128)(4,1)}, u32[]{:S(2)}) copy-start(pred[320]{0:T(512)(128)(4,1)} %get-tuple-element.354) | copy-start | bytes 964
  (100 other events, 699.8 us)
where the time goes:
time: 570 us; the launch traced here: 567 us
  blocking collectives  410 us (72%)
  local copies, waits for them, and re-layouts  94 us (16%)
  other arithmetic  34.3 us (6%)
  starting transfers between devices  17 us (3%)
  between operations  9.18 us (2%)
    psum x1, blocking collectives, on_device(): coarse_rhs = lax.psum(coarse_partial, ('gx', 'gy'))  109 us
    psum x1, blocking collectives, on_device(): lax.psum((precond_local, curvature_local, norm_local), ('gx', 'gy'))  102 us
    unnamed x1, blocking collectives  99.5 us
    psum x1, blocking collectives, on_device(): fresh_norm = lax.psum(jnp.sum(residual_out * residual_out), ('gx', 'gy'))  99.4 us
    mul x78, local copies, waits for them, and re-layouts, contract(): total = total + matrices[index][:, None, None, :] * moved[index][None]  28.3 us
    unnamed x280, local copies, waits for them, and re-layouts  12 us
    all_to_all x2, starting transfers between devices, face_sum(): lax.all_to_all(outgoing, 'gy', split_axis=1, concat_axis=1, tiled=True)  11.8 us
  transfers between devices with their start and end apart: 6, of which 0 were waited for; matrix products, arithmetic and copies ran while one was open for 12% of the time, Pallas kernels for 0%

commit v1 on v0

--- a/solution.py
+++ b/solution.py
@@ -191,7 +191,7 @@
     coarse_partial = jax.ops.segment_sum(
         corners.reshape(-1), vertex_ids.reshape(-1), num_segments=coarse_inverse.shape[1]
     )
-    coarse_rhs = lax.psum(coarse_partial, ("gx", "gy"))
+    coarse_rhs = jnp.sum(lax.all_gather(coarse_partial, ("gx", "gy")), axis=0)
     own_values = jnp.dot(coarse_inverse, coarse_rhs, precision=top_precision)
     coarse_sol = lax.all_gather(own_values, ("gx", "gy"), axis=0, tiled=True)
     smooth = fdm_solve(rmask.reshape(EDGE, EDGE, EDGE, -1), fdm_vectors, fdm_values).reshape(

time: 570 us -> 650 us (1.14)
  waiting for transfers between devices: 0.02 us -> 152 us
  blocking collectives: 410 us -> 304 us
  local copies, waits for them, and re-layouts: 94 us -> 108 us
  between operations: 9.18 us -> 22.7 us
    all_gather x0 -> x1, waiting for transfers between devices: none -> 152 us  [on_device(): coarse_rhs = jnp.sum(lax.all_gather(coarse_partial, ('gx', 'gy')), axis=0)]
    psum x1 -> x0, blocking collectives: 109 us -> none  [on_device(): coarse_rhs = lax.psum(coarse_partial, ('gx', 'gy'))]
    all_gather x0 -> x1, local copies, waits for them, and re-layouts: none -> 18.2 us  [on_device(): coarse_rhs = jnp.sum(lax.all_gather(coarse_partial, ('gx', 'gy')), axis=0)]
    reduce_sum x0 -> x1, other arithmetic: none -> 6.55 us  [on_device(): coarse_rhs = jnp.sum(lax.all_gather(coarse_partial, ('gx', 'gy')), axis=0)]
  transfers between devices with their start and end apart: 6 -> 7, of which waited for: 0 -> 1; matrix products, arithmetic and copies ran while one was open for 12% -> 13% of each run, Pallas kernels for 0% -> 0%
where the time goes in v1:
time: 650 us; the launch traced here: 647 us
  blocking collectives  304 us (47%)
  waiting for transfers between devices  152 us (23%)
  local copies, waits for them, and re-layouts  108 us (17%)
  other arithmetic  40.2 us (6%)
  between operations  22.7 us (3%)
  starting transfers between devices  16.5 us (3%)
    all_gather x1, waiting for transfers between devices, on_device(): coarse_rhs = jnp.sum(lax.all_gather(coarse_partial, ('gx', 'gy')), axis=0)  152 us
    psum x1, blocking collectives, on_device(): lax.psum((precond_local, curvature_local, norm_local), ('gx', 'gy'))  103 us
    unnamed x1, blocking collectives  101 us
    psum x1, blocking collectives, on_device(): fresh_norm = lax.psum(jnp.sum(residual_out * residual_out), ('gx', 'gy'))  99.4 us
    mul x78, local copies, waits for them, and re-layouts, contract(): total = total + matrices[index][:, None, None, :] * moved[index][None]  28.6 us
    all_gather x1, local copies, waits for them, and re-layouts, on_device(): coarse_rhs = jnp.sum(lax.all_gather(coarse_partial, ('gx', 'gy')), axis=0)  18.2 us
  transfers between devices with their start and end apart: 7, of which 1 were waited for; matrix products, arithmetic and copies ran while one was open for 13% of the time, Pallas kernels for 0%

profile of v1, /device:TPU:1, one launch (start us, length us, event | category | flops | bytes accessed | tf_op | source)
XLA Modules:
  0.0 646.7 jit_solution(8673974330292471463)
XLA Ops:
  9.6 6.6 %scatter_custom_fusion.1 = f32[8192]{0:T(1024)} fusion(s32[1024]{0:T(1024)} %bitcast.649, f32[1024]{0:T(1024)S(1)} %convolution_bitcast_fusion, f32[]{:T(128)} %constant.402.clone.1), kind=kCustom, calls=%fused_computation.199 | custom fusion | flops 1024 | bytes 33280 | tf_op jit(solution)/shard_map/scatter-add | solution.py:191
  21.4 2.3 copy.389
  23.7 2.5 reshape.1869
  29.9 7.6 %all-to-all-start = ((f32[16,1,1280]{2,1,0:T(1,128)}), f32[16,1,1280]{2,1,0:T(1,128)}, u32[]{:S(2)}, u32[]{:S(2)}) async-start(f32[16,1,1280]{2,1,0:T(1,128)} %reshape.1991), calls=%async_computation | async-start | bytes 163840 | tf_op jit(solution)/shard_map/all_to_all | solution.py:137
  38.5 2.5 collective-permute-start
  69.6 1.7 reduce.26
  72.5 2.5 scatter_custom_fusion
  75.0 2.6 reshape.1876
  77.6 3.4 fusion.54
  81.1 1.2 copy.456
  82.3 1.2 copy.457
  83.5 1.2 copy.401
  84.8 1.2 copy.403
  89.6 152.3 %all-gather.3.cloned.1.call-done = f32[4194304]{0:T(1024)} async-done(((f32[8192]{0:T(1024)}), f32[4194304]{0:T(1024)}) %all-gather.3.cloned.1.call-update) | async-done | bytes 16777232 | tf_op jit(solution)/shard_map/all_gather | solution.py:194
  241.9 18.2 %reshape.1965 = f32[512,8192]{1,0:T(8,128)} reshape(f32[4194304]{0:T(1024)} %all-gather.3.cloned.1.call-done) | data formatting | bytes 33554432 | tf_op jit(solution)/shard_map/all_gather | solution.py:194
  260.2 6.5 %reduce_sum.63 = f32[8192]{0:T(1024)S(1)} reduce(f32[512,8192]{1,0:T(8,128)} %reshape.1965, f32[]{:T(128)} %constant.402.clone.1), dimensions={0}, to_apply=%region_2.5 | reduce | flops 4186112 | bytes 16809988 | tf_op jit(solution)/shard_map/reduce_sum | solution.py:194
  267.7 101.2 %all-reduce = f32[8192]{0:T(1024)S(1)} all-reduce(f32[8192]{0:T(1024)S(1)} %dynamic-update-slice.36), channel_id=1, replica_groups=mesh['gx'=32,'gy'=16] {'gx','gy'}, use_global_device_ids=true, to_apply=%add | all-reduce | flops 8192 | bytes 65536
  368.9 6.2 gather_fusion
  375.2 2.3 multiply_reduce_fusion
  378.0 1.7 multiply_add_fusion
  382.7 2.3 copy.428
  385.0 2.4 reshape.1886
  390.3 4.4 all-to-all-start.1
  412.0 2.9 add_reduce_fusion
  416.2 103.0 %all-reduce.2 = (f32[]{:T(128)}, f32[]{:T(128)}) all-reduce(f32[]{:T(128)} %get-tuple-element.150, f32[]{:T(128)S(6)} %add.968), channel_id=1, replica_groups=mesh['gx'=32,'gy'=16] {'gx','gy'}, use_global_device_ids=true, to_apply=%region_4.7 | all-reduce | flops 2 | bytes 16 | tf_op jit(solution)/shard_map/psum | solution.py:207
  520.4 1.7 add_multiply_fusion
  523.1 1.7 reduce.27
  526.0 2.3 scatter_custom_fusion.2
  528.3 2.6 reshape.1893
  530.9 2.9 fusion.53
  536.7 1.3 multiply_reduce_fusion.1
  538.1 99.4 %all-reduce.1 = (f32[]{:T(128)}, f32[]{:T(128)}) all-reduce(f32[]{:T(128)} %get-tuple-element.156, f32[]{:T(128)} %get-tuple-element.149), channel_id=1, replica_groups=mesh['gx'=32,'gy'=16] {'gx','gy'}, use_global_device_ids=true, to_apply=%region_11.14 | all-reduce | flops 2 | bytes 16 | tf_op jit(solution)/shard_map/psum | solution.py:212
  (539 shorter events, 72.3 us)
Async XLA Ops:
  7.2 259.6 %copy-start = (f32[16,8192]{1,0:T(8,128)S(1)}, f32[16,8192]{1,0:T(8,128)}, u32[]{:S(2)}) copy-start(f32[16,8192]{1,0:T(8,128)} %param.48) | copy-start | bytes 1572868
  7.2 234.8 %all-gather.3.cloned.1.call-start = ((), (), s32[]{:S(2)}) async-start(), calls=%async_computation.2 | async-start | bytes 16809984 | tf_op jit(solution)/shard_map/all_gather | solution.py:194
  23.7 22.2 %copy-start.2 = (bf16[3,512,128]{2,1,0:T(8,128)(2,1)S(1)}, bf16[3,512,128]{2,1,0:T(8,128)(2,1)}, u32[]{:S(2)}) copy-start(bf16[3,512,128]{2,1,0:T(8,128)(2,1)} %param.44) | copy-start | bytes 1179652
  26.2 20.7 %copy-start.1 = (bf16[3,512,128]{2,1,0:T(8,128)(2,1)S(1)}, bf16[3,512,128]{2,1,0:T(8,128)(2,1)}, u32[]{:S(2)}) copy-start(bf16[3,512,128]{2,1,0:T(8,128)(2,1)} %param.43) | copy-start | bytes 1179652
  26.6 21.2 %copy-start.120 = (s32[1024]{0:T(1024)}, s32[1024]{0:T(1024)S(1)}, u32[]{:S(2)}) copy-start(s32[1024]{0:T(1024)S(1)} %get-tuple-element.373) | copy-start | bytes 12292
  29.9 39.1 %all-to-all-start = ((f32[16,1,1280]{2,1,0:T(1,128)}), f32[16,1,1280]{2,1,0:T(1,128)}, u32[]{:S(2)}, u32[]{:S(2)}) async-start(f32[16,1,1280]{2,1,0:T(1,128)} %reshape.1991), calls=%async_computation | async-start | bytes 163840 | tf_op jit(solution)/shard_map/all_to_all | solution.py:137
  38.3 30.7 %copy-start.70 = (pred[128]{0:T(512)(128)(4,1)}, pred[128]{0:T(512)(128)(4,1)S(1)}, u32[]{:S(2)}) copy-start(pred[128]{0:T(512)(128)(4,1)S(1)} %get-tuple-element.360) | copy-start | bytes 388
  38.3 30.7 %copy-start.93 = (pred[128]{0:T(512)(128)(4,1)}, pred[128]{0:T(512)(128)(4,1)S(1)}, u32[]{:S(2)}) copy-start(pred[128]{0:T(512)(128)(4,1)S(1)} %get-tuple-element.361) | copy-start | bytes 388
  38.3 30.7 %copy-start.127 = (pred[128]{0:T(512)(128)(4,1)}, pred[128]{0:T(512)(128)(4,1)S(1)}, u32[]{:S(2)}) copy-start(pred[128]{0:T(512)(128)(4,1)S(1)} %get-tuple-element.359) | copy-start | bytes 388
  38.5 30.3 %collective-permute-start = (f32[64,1,64]{2,0,1:T(8,128)S(1)}, f32[64,1,64]{2,0,1:T(8,128)S(1)}, u32[]{:S(2)}, u32[]{:S(2)}) collective-permute-start(f32[64,1,64]{2,0,1:T(8,128)S(1)} %copy.454), channel_id=1, source_target_pairs={{0,16},{16,32},{32,48},{48,64},{64,80},{80,96},{96,112},{112,128},... | collective-permute-start | bytes 49160 | tf_op jit(solution)/shard_map/ppermute | solution.py:16
  41.1 27.8 %collective-permute-start.1 = (f32[64,1,64]{2,0,1:T(8,128)S(1)}, f32[64,1,64]{2,0,1:T(8,128)S(1)}, u32[]{:S(2)}, u32[]{:S(2)}) collective-permute-start(f32[64,1,64]{2,0,1:T(8,128)S(1)} %copy.455), channel_id=1, source_target_pairs={{16,0},{32,16},{48,32},{64,48},{80,64},{96,80},{112,96},{128,112},... | collective-permute-start | bytes 49160 | tf_op jit(solution)/shard_map/ppermute | solution.py:19
  43.8 20.9 %copy-start.53 = (f32[8]{0:T(128)}, f32[8]{0:T(128)S(1)}, u32[]{:S(2)}) copy-start(f32[8]{0:T(128)S(1)} %get-tuple-element.352) | copy-start | bytes 100
  43.8 21.6 %copy-start.51 = (f32[8]{0:T(128)}, f32[8]{0:T(128)S(1)}, u32[]{:S(2)}) copy-start(f32[8]{0:T(128)S(1)} %get-tuple-element.351) | copy-start | bytes 100
  43.8 22.3 %copy-start.49 = (f32[8]{0:T(128)}, f32[8]{0:T(128)S(1)}, u32[]{:S(2)}) copy-start(f32[8]{0:T(128)S(1)} %get-tuple-element.350) | copy-start | bytes 100
  43.8 22.9 %copy-start.47 = (f32[8]{0:T(128)}, f32[8]{0:T(128)S(1)}, u32[]{:S(2)}) copy-start(f32[8]{0:T(128)S(1)} %get-tuple-element.349) | copy-start | bytes 100
  43.8 23.6 %copy-start.45 = (f32[8]{0:T(128)}, f32[8]{0:T(128)S(1)}, u32[]{:S(2)}) copy-start(f32[8]{0:T(128)S(1)} %get-tuple-element.348) | copy-start | bytes 100
  43.9 24.3 %copy-start.43 = (f32[8]{0:T(128)}, f32[8]{0:T(128)S(1)}, u32[]{:S(2)}) copy-start(f32[8]{0:T(128)S(1)} %get-tuple-element.347) | copy-start | bytes 100
  51.5 20.8 %copy-start.83 = (pred[320]{0:T(512)(128)(4,1)S(1)}, pred[320]{0:T(512)(128)(4,1)}, u32[]{:S(2)}) copy-start(pred[320]{0:T(512)(128)(4,1)} %get-tuple-element.356) | copy-start | bytes 964
  51.5 20.8 %copy-start.121 = (pred[320]{0:T(512)(128)(4,1)S(1)}, pred[320]{0:T(512)(128)(4,1)}, u32[]{:S(2)}) copy-start(pred[320]{0:T(512)(128)(4,1)} %get-tuple-element.354) | copy-start | bytes 964
  260.2 108.7 %copy-start.79 = (s32[1024]{0:T(1024)S(1)}, s32[1024]{0:T(1024)}, u32[]{:S(2)}) copy-start(s32[1024]{0:T(1024)} %fusion.40) | copy-start | bytes 12292
  266.7 108.4 %copy-start.81 = (f32[128]{0:T(128)S(1)}, f32[128]{0:T(128)}, u32[]{:S(2)}) copy-start(f32[128]{0:T(128)} %copy-done.80) | copy-start | bytes 1540
  390.3 132.8 %all-to-all-start.1 = ((f32[16,1,1280]{2,1,0:T(1,128)}), f32[16,1,1280]{2,1,0:T(1,128)}, u32[]{:S(2)}, u32[]{:S(2)}) async-start(f32[16,1,1280]{2,1,0:T(1,128)} %reshape.1993), calls=%async_computation.1 | async-start | bytes 163840 | tf_op jit(solution)/shard_map/all_to_all | solution.py:137
  395.5 126.6 %collective-permute-start.2 = (f32[64,1,64]{2,0,1:T(8,128)}, f32[64,1,64]{2,0,1:T(8,128)}, u32[]{:S(2)}, u32[]{:S(2)}) collective-permute-start(f32[64,1,64]{2,0,1:T(8,128)} %copy.460), channel_id=1, source_target_pairs={{0,16},{16,32},{32,48},{48,64},{64,80},{80,96},{96,112},{112,128},... | collective-permute-start | bytes 49160 | tf_op jit(solution)/shard_map/ppermute | solution.py:16
  397.2 124.9 %collective-permute-start.3 = (f32[64,1,64]{2,0,1:T(8,128)}, f32[64,1,64]{2,0,1:T(8,128)}, u32[]{:S(2)}, u32[]{:S(2)}) collective-permute-start(f32[64,1,64]{2,0,1:T(8,128)} %copy.461), channel_id=1, source_target_pairs={{16,0},{32,16},{48,32},{64,48},{80,64},{96,80},{112,96},{128,112},... | collective-permute-start | bytes 49160 | tf_op jit(solution)/shard_map/ppermute | solution.py:19
  412.0 108.4 %copy-start.82 = (f32[128]{0:T(128)S(1)}, f32[128]{0:T(128)}, u32[]{:S(2)}) copy-start(f32[128]{0:T(128)} %copy-done.80) | copy-start | bytes 1540
  412.0 111.0 %copy-start.71 = (pred[128]{0:T(512)(128)(4,1)S(1)}, pred[128]{0:T(512)(128)(4,1)}, u32[]{:S(2)}) copy-start(pred[128]{0:T(512)(128)(4,1)} %copy-done.70) | copy-start | bytes 388
  412.0 111.0 %copy-start.94 = (pred[128]{0:T(512)(128)(4,1)S(1)}, pred[128]{0:T(512)(128)(4,1)}, u32[]{:S(2)}) copy-start(pred[128]{0:T(512)(128)(4,1)} %copy-done.93) | copy-start | bytes 388
  412.0 111.0 %copy-start.128 = (pred[128]{0:T(512)(128)(4,1)S(1)}, pred[128]{0:T(512)(128)(4,1)}, u32[]{:S(2)}) copy-start(pred[128]{0:T(512)(128)(4,1)} %copy-done.127) | copy-start | bytes 388
  412.0 112.9 %copy-start.133 = (pred[16]{0:T(512)(128)(4,1)S(1)}, pred[16]{0:T(512)(128)(4,1)}, u32[]{:S(2)}) copy-start(pred[16]{0:T(512)(128)(4,1)} %iota_compare_fusion.2) | copy-start | bytes 52
  414.9 110.7 %copy-start.69 = (pred[320]{0:T(512)(128)(4,1)S(1)}, pred[320]{0:T(512)(128)(4,1)}, u32[]{:S(2)}) copy-start(pred[320]{0:T(512)(128)(4,1)} %get-tuple-element.355) | copy-start | bytes 964
  414.9 110.9 %copy-start.84 = (pred[320]{0:T(512)(128)(4,1)S(1)}, pred[320]{0:T(512)(128)(4,1)}, u32[]{:S(2)}) copy-start(pred[320]{0:T(512)(128)(4,1)} %get-tuple-element.356) | copy-start | bytes 964
  414.9 110.9 %copy-start.122 = (pred[320]{0:T(512)(128)(4,1)S(1)}, pred[320]{0:T(512)(128)(4,1)}, u32[]{:S(2)}) copy-start(pred[320]{0:T(512)(128)(4,1)} %get-tuple-element.354) | copy-start | bytes 964
  (111 other events, 832.6 us)
Sparse Core Ops, SparseCore 0:
  16.4 225.5 all-gather.2
